TPU v7x, 256 devices: a whole 4x4x8 slice. The times are simulated.
256 devices in a mesh: dp: 16 (over y, x), expert: 16 (over z, core).
Axes of the slice: x: 4, y: 4, z: 8, core: 2. Of those that a mesh axis runs over, the one named last changes fastest.
Arguments:
- tokens: bfloat16 [16384, 2048], P(('dp', 'expert')), may hold values from -6 to 6
- expert_ids: int32 [16384, 10], P(('dp', 'expert')), may hold values from 0 to 255, all different within a row; in each aligned block of 64 rows (0 to 63, 64 to 127, ...) at most 3 rows name the same one
- gate_probs: float32 [16384, 10], P(('dp', 'expert')), may hold values from 0.03 to 0.3
- w_gate: bfloat16 [256, 2048, 512], P(('dp', 'expert')), may hold values from -0.125 to 0.125
- w_up: bfloat16 [256, 2048, 512], P(('dp', 'expert')), may hold values from -0.125 to 0.125
- w_down: bfloat16 [256, 512, 2048], P(('dp', 'expert')), may hold values from -0.25 to 0.25
- grad_out: bfloat16 [16384, 2048], P(('dp', 'expert')), may hold values from -6 to 6
Outputs:
- mixed: bfloat16 [16384, 2048], P(('dp', 'expert'))
- grad_tokens: bfloat16 [16384, 2048], P(('dp', 'expert'))
- grad_probs: float32 [16384, 10], P(('dp', 'expert'))
Inputs may be any that keep to these rules, and one draw needn't show every extreme that they name: `expert_ids`: the 10 experts of a token differ. Among the 64 consecutive tokens of one device (aligned blocks), no expert is named more than 3 times.
All inputs are finite; a program needn't handle non-finite values.
Results may differ from a plain program's by a relative error of at most 0.0064.
Values may be sent and summed in bfloat16 or wider, within the bound.
No kernel may reach another device: no remote copies, remote signals or barrier semaphores. Data moves between devices by JAX's collectives and lax.ppermute only.
A program may use at most 128 MiB of HBM per device.

v0:
```python
import jax
import jax.numpy as jnp
from jax import lax
from jax.sharding import PartitionSpec as P


def expert_forward(rows, wg, wu, wd):
    pre_gate = jnp.dot(rows, wg, preferred_element_type=jnp.float32)
    pre_up = jnp.dot(rows, wu, preferred_element_type=jnp.float32)
    hidden = (jax.nn.silu(pre_gate) * pre_up).astype(jnp.bfloat16)
    return jnp.dot(hidden, wd, preferred_element_type=jnp.float32).astype(jnp.bfloat16)


def backward_from(pre_gate, pre_up, scaled, wg, wu, wd):
    sig = jax.nn.sigmoid(pre_gate)
    grad_hidden = lax.dot_general(
        scaled, wd, (((1,), (1,)), ((), ())), preferred_element_type=jnp.float32
    )
    grad_gate = (grad_hidden * pre_up * sig * (1.0 + pre_gate * (1.0 - sig))).astype(jnp.bfloat16)
    grad_up = (grad_hidden * pre_gate * sig).astype(jnp.bfloat16)
    total = lax.dot_general(
        grad_gate, wg, (((1,), (1,)), ((), ())), preferred_element_type=jnp.float32
    )
    total = total + lax.dot_general(
        grad_up, wu, (((1,), (1,)), ((), ())), preferred_element_type=jnp.float32
    )
    return total.astype(jnp.bfloat16)


def expert_backward(rows, scaled, wg, wu, wd):
    pre_gate = jnp.dot(rows, wg, preferred_element_type=jnp.float32)
    pre_up = jnp.dot(rows, wu, preferred_element_type=jnp.float32)
    return backward_from(pre_gate, pre_up, scaled, wg, wu, wd)


def through_owners(payload, work):
    arrived = lax.all_to_all(
        lax.all_to_all(payload, "dp", split_axis=1, concat_axis=1, tiled=True),
        "expert",
        split_axis=2,
        concat_axis=2,
        tiled=True,
    )
    middle = lax.all_to_all(work(arrived), "expert", split_axis=1, concat_axis=1, tiled=True)
    return lax.all_to_all(middle, "dp", split_axis=0, concat_axis=0, tiled=True)


def body(tokens, expert_ids, gate_probs, w_gate, w_up, w_down, grad_out):
    tok_dev, top = expert_ids.shape
    width = tokens.shape[1]
    n_data = lax.axis_size("dp")
    n_owner = lax.axis_size("expert")
    experts = n_data * n_owner
    most = max(3, (6 * tok_dev * top + 5 * experts - 1) // (5 * experts))
    flat = expert_ids.reshape(-1)
    entries = flat.shape[0]
    onehot = flat[:, None] == jnp.arange(experts, dtype=jnp.int32)[None, :]
    positions = jnp.arange(entries, dtype=jnp.int32)
    before = (positions[:, None] > positions[None, :]).astype(jnp.bfloat16)
    earlier = jnp.dot(before, onehot.astype(jnp.bfloat16), preferred_element_type=jnp.float32)
    slot = jnp.sum(jnp.where(onehot, earlier, 0.0), axis=1).astype(jnp.int32)
    target = flat * most + slot
    weight_gate = w_gate[0]
    weight_up = w_up[0]
    weight_down = w_down[0]
    row_copies = jnp.repeat(tokens, top, axis=0)
    buffer = jnp.zeros((experts * most, width), jnp.bfloat16).at[target].set(row_copies)
    scaled = (gate_probs[:, :, None] * grad_out[:, None, :].astype(jnp.float32)).astype(
        jnp.bfloat16
    )
    scaled_buf = (
        jnp.zeros((experts * most, width), jnp.bfloat16).at[target].set(scaled.reshape(-1, width))
    )
    both = jnp.stack([buffer, scaled_buf]).reshape(2, n_data, n_owner, most, width)

    def forward_work(parts):
        shape = parts.shape
        rows = parts[0].reshape(-1, width)
        result = expert_forward(rows, weight_gate, weight_up, weight_down)
        return result.reshape(shape[1:])

    sent = buffer.reshape(1, n_data, n_owner, most, width)
    routed_buf = through_owners(sent, forward_work).reshape(experts * most, width)

    def backward_work(parts):
        shape = parts.shape
        rows = parts[0].reshape(-1, width)
        cotan = parts[1].reshape(-1, width)
        result = expert_backward(rows, cotan, weight_gate, weight_up, weight_down)
        return result.reshape(shape[1:])

    back_buf = through_owners(both, backward_work).reshape(experts * most, width)
    routed = routed_buf[target].reshape(tok_dev, top, width)
    mixed = jnp.sum(gate_probs[:, :, None] * routed.astype(jnp.float32), axis=1).astype(
        jnp.bfloat16
    )
    grad_probs = jnp.sum(
        grad_out[:, None, :].astype(jnp.float32) * routed.astype(jnp.float32), axis=2
    )
    back_rows = back_buf[target].reshape(tok_dev, top, width)
    grad_tokens = jnp.sum(back_rows.astype(jnp.float32), axis=1).astype(jnp.bfloat16)
    return (mixed, grad_tokens, grad_probs)


def solution(mesh):
    return jax.shard_map(
        body,
        mesh=mesh,
        in_specs=(
            P(("dp", "expert"), None),
            P(("dp", "expert"), None),
            P(("dp", "expert"), None),
            P(("dp", "expert"), None, None),
            P(("dp", "expert"), None, None),
            P(("dp", "expert"), None, None),
            P(("dp", "expert"), None),
        ),
        out_specs=(P(("dp", "expert"), None), P(("dp", "expert"), None), P(("dp", "expert"), None)),
        check_vma=False,
    )
```

profile of v0, /device:TPU:32, one launch (start us, length us, event | category | flops | bytes accessed | tf_op | source)
XLA Modules:
  0.0 719.8 jit_solution(1014203727731716796)
XLA Ops:
  12.1 9.9 %scatter_custom_fusion = bf16[768,2048]{1,0:T(8,128)(2,1)} fusion(s32[640]{0:T(1024)S(1)} %fusion.33, bf16[640,2048]{1,0:T(8,128)(2,1)} %reshape.113, bf16[]{:T(256)} %constant.6.clone.1), kind=kCustom, calls=%fused_computation.33 | custom fusion | bytes 3146240 | tf_op jit(solution)/shard_map/scatter | solution.py:67
  22.0 9.1 %reshape.86 = bf16[1,16,16,3,2048]{4,3,2,1,0:T(4,128)(2,1)} reshape(bf16[768,2048]{1,0:T(8,128)(2,1)} %scatter_custom_fusion) | data formatting | bytes 6291456 | tf_op jit(solution)/shard_map/reshape | solution.py:82
  37.5 7.7 %all-to-all-start = ((bf16[1,16,16,3,2048]{4,2,3,0,1:T(8,128)(2,1)}), bf16[1,16,16,3,2048]{4,2,3,0,1:T(8,128)(2,1)}, u32[]{:S(2)}, u32[]{:S(2)}) async-start(bf16[1,16,16,3,2048]{4,2,3,0,1:T(8,128)(2,1)} %copy.18), calls=%async_computation | async-start | bytes 6291456 | tf_op jit(solution)/shard_map/all_to_all | solution.py:38
  49.8 7.4 %mul.87 = f32[640,2048]{1,0:T(8,128)} reshape(f32[64,10,2048]{2,1,0:T(8,128)} %mul.86) | data formatting | bytes 10485760 | tf_op jit(solution)/shard_map/mul | solution.py:68
  57.2 14.1 %scatter_custom_fusion.1 = bf16[768,2048]{1,0:T(8,128)(2,1)} fusion(s32[640]{0:T(1024)S(1)} %fusion.33, f32[640,2048]{1,0:T(8,128)} %mul.87, f32[640]{0:T(1024)S(1)} %mul.84, bf16[]{:T(256)} %constant.6.clone.1), kind=kCustom, calls=%fused_computation.10 | custom fusion | flops 2621440 | bytes 8392706 | tf_op jit(solution)/shard_map/scatter | solution.py:72
  71.3 9.1 %stack.7 = bf16[1,16,16,3,2048]{4,3,2,1,0:T(4,128)(2,1)} reshape(bf16[768,2048]{1,0:T(8,128)(2,1)} %scatter_custom_fusion.1) | data formatting | bytes 6291456 | tf_op jit(solution)/shard_map/stack | solution.py:74
  80.4 7.6 %pad_maximum_fusion = bf16[2,16,16,3,2048]{4,3,2,1,0:T(4,128)(2,1)S(1)} fusion(bf16[1,16,16,3,2048]{4,3,2,1,0:T(4,128)(2,1)} %stack.7, bf16[1,16,16,3,2048]{4,3,2,1,0:T(4,128)(2,1)} %reshape.86), kind=kLoop, calls=%fused_computation.4 | loop fusion | flops 3145728 | bytes 12582912 | tf_op jit(solution)/shard_map/stack | solution.py:74
  88.0 9.1 %copy.25 = bf16[2,16,16,3,2048]{4,2,3,0,1:T(8,128)(2,1)} copy(bf16[2,16,16,3,2048]{4,3,2,1,0:T(4,128)(2,1)S(1)} %pad_maximum_fusion) | data formatting | bytes 12582912 | tf_op jit(solution)/shard_map/stack | solution.py:74
  97.2 7.4 %all-to-all-start.4 = ((bf16[2,16,16,3,2048]{4,2,3,0,1:T(8,128)(2,1)}), bf16[2,16,16,3,2048]{4,2,3,0,1:T(8,128)(2,1)}, u32[]{:S(2)}, u32[]{:S(2)}) async-start(bf16[2,16,16,3,2048]{4,2,3,0,1:T(8,128)(2,1)} %copy.25), calls=%async_computation.4 | async-start | bytes 12582912 | tf_op jit(solution)/shard_map/all_to_all | solution.py:38
  109.8 87.3 %all-to-all-done.4 = bf16[2,16,16,3,2048]{4,2,3,0,1:T(8,128)(2,1)} async-done(((bf16[2,16,16,3,2048]{4,2,3,0,1:T(8,128)(2,1)}), bf16[2,16,16,3,2048]{4,2,3,0,1:T(8,128)(2,1)}, u32[]{:S(2)}, u32[]{:S(2)}) %all-to-all-start.4) | async-done | bytes 6291488 | tf_op jit(solution)/shard_map/all_to_all | solution.py:38
  197.1 9.1 %all-to-all-start.1 = ((bf16[1,16,16,3,2048]{4,1,3,0,2:T(8,128)(2,1)}), bf16[1,16,16,3,2048]{4,1,3,0,2:T(8,128)(2,1)}, u32[]{:S(2)}, u32[]{:S(2)}) async-start(bf16[1,16,16,3,2048]{4,1,3,0,2:T(8,128)(2,1)} %copy.19), calls=%async_computation.1 | async-start | bytes 6291456 | tf_op jit(solution)/shard_map/all_to_all | solution.py:37
  206.2 8.9 %copy.26 = bf16[2,16,16,3,2048]{4,1,3,0,2:T(8,128)(2,1)} copy(bf16[2,16,16,3,2048]{4,2,3,0,1:T(8,128)(2,1)} %all-to-all-done.4) | data formatting | bytes 12582912 | tf_op jit(solution)/shard_map/all_to_all | solution.py:38
  215.1 61.0 %all-to-all-done.1 = bf16[1,16,16,3,2048]{4,1,3,0,2:T(8,128)(2,1)} async-done(((bf16[1,16,16,3,2048]{4,1,3,0,2:T(8,128)(2,1)}), bf16[1,16,16,3,2048]{4,1,3,0,2:T(8,128)(2,1)}, u32[]{:S(2)}, u32[]{:S(2)}) %all-to-all-start.1) | async-done | bytes 3145760 | tf_op jit(solution)/shard_map/all_to_all | solution.py:37
  289.1 8.8 %reshape_squeeze.9 = bf16[768,2048]{1,0:T(8,128)(2,1)} reshape(bf16[1,16,16,3,2048]{4,3,2,1,0:T(4,128)(2,1)} %copy.20) | data formatting | bytes 6291456 | tf_op jit(solution)/shard_map/reshape;squeeze | solution.py:78
  303.5 8.2 %convolution_convert_fusion = bf16[768,2048]{1,0:T(8,128)(2,1)} fusion(bf16[1,512,2048]{2,1,0:T(8,128)(2,1)} %param.12, f32[768,512]{1,0:T(8,128)} %fusion.14, bf16[768,2048]{1,0:T(8,128)(2,1)} %reshape_squeeze.9, bf16[1,2048,512]{2,1,0:T(8,128)(2,1)S(1)} %copy-done), kind=kOutput, calls=%fused_computation.9 | convolution fusion | flops 3225157632 | bytes 12058624 | tf_op jit(solution)/shard_map/dot_general | solution.py:11
  311.7 9.1 %reshape.87 = bf16[16,16,3,2048]{3,2,1,0:T(4,128)(2,1)} reshape(bf16[768,2048]{1,0:T(8,128)(2,1)} %convolution_convert_fusion) | data formatting | bytes 6291456 | tf_op jit(solution)/shard_map/reshape | solution.py:80
  327.1 92.9 %all-to-all-done.5 = bf16[2,16,16,3,2048]{4,1,3,0,2:T(8,128)(2,1)} async-done(((bf16[2,16,16,3,2048]{4,1,3,0,2:T(8,128)(2,1)}), bf16[2,16,16,3,2048]{4,1,3,0,2:T(8,128)(2,1)}, u32[]{:S(2)}, u32[]{:S(2)}) %all-to-all-start.5) | async-done | bytes 6291488 | tf_op jit(solution)/shard_map/all_to_all | solution.py:37
  420.0 6.9 all-to-all-start.2
  437.0 8.8 %reshape_squeeze.10 = bf16[768,2048]{1,0:T(8,128)(2,1)} reshape(bf16[1,16,16,3,2048]{4,3,2,1,0:T(4,128)(2,1)} %copy.27) | data formatting | bytes 6291456 | tf_op jit(solution)/shard_map/reshape;squeeze | solution.py:88
  452.3 8.8 %reshape_squeeze.11 = bf16[768,2048]{1,0:T(8,128)(2,1)} reshape(bf16[1,16,16,3,2048]{4,3,2,1,0:T(4,128)(2,1)} %copy.28) | data formatting | bytes 6291456 | tf_op jit(solution)/shard_map/reshape;squeeze | solution.py:87
  469.7 9.9 %fusion.10 = f32[768,2048]{1,0:T(8,128)} fusion(bf16[1,2048,512]{2,1,0:T(8,128)(2,1)} %param.10, f32[768,512]{1,0:T(8,128)} %fusion.12, f32[768,512]{1,0:T(8,128)} %fusion.2, bf16[768,2048]{1,0:T(8,128)(2,1)} %reshape_squeeze.11, bf16[1,2048,512]{2,1,0:T(8,128)(2,1)S(1)} %copy-done), kind=kOutput, calls=%fused_computation.20 | convolution fusion | flops 3225157632 | bytes 16777216 | tf_op jit(solution)/shard_map/dot_general | solution.py:21
  479.6 7.2 %add_convert_fusion = bf16[768,2048]{1,0:T(8,128)(2,1)} fusion(f32[768,2048]{1,0:T(8,128)} %fusion.10, bf16[1,2048,512]{2,1,0:T(8,128)(2,1)S(1)} %copy-done, f32[768,512]{1,0:T(8,128)} %fusion.2, f32[768,512]{1,0:T(8,128)} %fusion.12), kind=kOutput, calls=%fused_computation.7 | convolution fusion | flops 1616117760 | bytes 14680064 | tf_op jit(solution)/shard_map/dot_general | solution.py:24
  486.8 9.1 %reshape.89 = bf16[16,16,3,2048]{3,2,1,0:T(4,128)(2,1)} reshape(bf16[768,2048]{1,0:T(8,128)(2,1)} %add_convert_fusion) | data formatting | bytes 6291456 | tf_op jit(solution)/shard_map/reshape | solution.py:90
  502.3 7.2 %all-to-all-start.6 = ((bf16[16,16,3,2048]{3,0,2,1:T(8,128)(2,1)}), bf16[16,16,3,2048]{3,0,2,1:T(8,128)(2,1)}, u32[]{:S(2)}, u32[]{:S(2)}) async-start(bf16[16,16,3,2048]{3,0,2,1:T(8,128)(2,1)} %copy.29), calls=%async_computation.6 | async-start | bytes 6291456 | tf_op jit(solution)/shard_map/all_to_all | solution.py:44
  514.8 64.6 %all-to-all-done.6 = bf16[16,16,3,2048]{3,0,2,1:T(8,128)(2,1)} async-done(((bf16[16,16,3,2048]{3,0,2,1:T(8,128)(2,1)}), bf16[16,16,3,2048]{3,0,2,1:T(8,128)(2,1)}, u32[]{:S(2)}, u32[]{:S(2)}) %all-to-all-start.6) | async-done | bytes 3145760 | tf_op jit(solution)/shard_map/all_to_all | solution.py:44
  589.9 43.5 %all-to-all-done.3 = bf16[16,16,3,2048]{3,1,2,0:T(8,128)(2,1)} async-done(((bf16[16,16,3,2048]{3,1,2,0:T(8,128)(2,1)}), bf16[16,16,3,2048]{3,1,2,0:T(8,128)(2,1)}, u32[]{:S(2)}, u32[]{:S(2)}) %all-to-all-start.3) | async-done | bytes 3145760 | tf_op jit(solution)/shard_map/all_to_all | solution.py:45
  638.3 6.6 copy.23
  644.9 8.8 %reshape.88 = bf16[768,2048]{1,0:T(8,128)(2,1)} reshape(bf16[16,16,3,2048]{3,2,1,0:T(4,128)(2,1)} %copy.23) | data formatting | bytes 6291456 | tf_op jit(solution)/shard_map/reshape | solution.py:83
  653.7 9.2 %gather_fusion = bf16[640,2048]{1,0:T(8,128)(2,1)} fusion(bf16[768,2048]{1,0:T(8,128)(2,1)} %reshape.88, s32[1024]{0:T(1024)S(1)} %pad_clamp_fusion), kind=kCustom, calls=%fused_computation | custom fusion | bytes 5245440 | tf_op jit(solution)/shard_map/gather | solution.py:93
  674.9 9.9 %all-to-all-done.7 = bf16[16,16,3,2048]{3,1,2,0:T(8,128)(2,1)} async-done(((bf16[16,16,3,2048]{3,1,2,0:T(8,128)(2,1)}), bf16[16,16,3,2048]{3,1,2,0:T(8,128)(2,1)}, u32[]{:S(2)}, u32[]{:S(2)}) %all-to-all-start.7) | async-done | bytes 3145760 | tf_op jit(solution)/shard_map/all_to_all | solution.py:45
  691.4 8.8 %reshape.90 = bf16[768,2048]{1,0:T(8,128)(2,1)} reshape(bf16[16,16,3,2048]{3,2,1,0:T(4,128)(2,1)} %copy.31) | data formatting | bytes 6291456 | tf_op jit(solution)/shard_map/reshape | solution.py:92
  700.2 9.4 %gather_fusion.1 = bf16[640,2048]{1,0:T(8,128)(2,1)} fusion(bf16[768,2048]{1,0:T(8,128)(2,1)} %reshape.90, s32[1024]{0:T(1024)S(1)} %pad_clamp_fusion), kind=kCustom, calls=%fused_computation.1 | custom fusion | bytes 5245440 | tf_op jit(solution)/shard_map/gather | solution.py:100
  (49 shorter events, 133.3 us)
Async XLA Ops:
  0.6 302.8 %copy-start = (bf16[1,2048,512]{2,1,0:T(8,128)(2,1)S(1)}, bf16[1,2048,512]{2,1,0:T(8,128)(2,1)}, u32[]{:S(2)}) copy-start(bf16[1,2048,512]{2,1,0:T(8,128)(2,1)} %param.11) | copy-start | bytes 6291460
  37.5 7.8 %copy-start.3 = (f32[64,10]{0,1:T(8,128)S(1)}, f32[64,10]{0,1:T(8,128)}, u32[]{:S(2)}) copy-start(f32[64,10]{0,1:T(8,128)} %param.9) | copy-start | bytes 7684
  37.5 8.0 %copy-start.2 = (bf16[64,2048]{1,0:T(8,128)(2,1)S(1)}, bf16[64,2048]{1,0:T(8,128)(2,1)}, u32[]{:S(2)}) copy-start(bf16[64,2048]{1,0:T(8,128)(2,1)} %param.13) | copy-start | bytes 786436
  37.5 59.7 %all-to-all-start = ((bf16[1,16,16,3,2048]{4,2,3,0,1:T(8,128)(2,1)}), bf16[1,16,16,3,2048]{4,2,3,0,1:T(8,128)(2,1)}, u32[]{:S(2)}, u32[]{:S(2)}) async-start(bf16[1,16,16,3,2048]{4,2,3,0,1:T(8,128)(2,1)} %copy.18), calls=%async_computation | async-start | bytes 6291456 | tf_op jit(solution)/shard_map/all_to_all | solution.py:38
  97.2 99.9 %all-to-all-start.4 = ((bf16[2,16,16,3,2048]{4,2,3,0,1:T(8,128)(2,1)}), bf16[2,16,16,3,2048]{4,2,3,0,1:T(8,128)(2,1)}, u32[]{:S(2)}, u32[]{:S(2)}) async-start(bf16[2,16,16,3,2048]{4,2,3,0,1:T(8,128)(2,1)} %copy.25), calls=%async_computation.4 | async-start | bytes 12582912 | tf_op jit(solution)/shard_map/all_to_all | solution.py:38
  197.1 79.0 %all-to-all-start.1 = ((bf16[1,16,16,3,2048]{4,1,3,0,2:T(8,128)(2,1)}), bf16[1,16,16,3,2048]{4,1,3,0,2:T(8,128)(2,1)}, u32[]{:S(2)}, u32[]{:S(2)}) async-start(bf16[1,16,16,3,2048]{4,1,3,0,2:T(8,128)(2,1)} %copy.19), calls=%async_computation.1 | async-start | bytes 6291456 | tf_op jit(solution)/shard_map/all_to_all | solution.py:37
  276.1 143.9 %all-to-all-start.5 = ((bf16[2,16,16,3,2048]{4,1,3,0,2:T(8,128)(2,1)}), bf16[2,16,16,3,2048]{4,1,3,0,2:T(8,128)(2,1)}, u32[]{:S(2)}, u32[]{:S(2)}) async-start(bf16[2,16,16,3,2048]{4,1,3,0,2:T(8,128)(2,1)} %copy.26), calls=%async_computation.5 | async-start | bytes 12582912 | tf_op jit(solution)/shard_map/all_to_all | solution.py:37
  420.0 82.2 %all-to-all-start.2 = ((bf16[16,16,3,2048]{3,0,2,1:T(8,128)(2,1)}), bf16[16,16,3,2048]{3,0,2,1:T(8,128)(2,1)}, u32[]{:S(2)}, u32[]{:S(2)}) async-start(bf16[16,16,3,2048]{3,0,2,1:T(8,128)(2,1)} %copy.21), calls=%async_computation.2 | async-start | bytes 6291456 | tf_op jit(solution)/shard_map/all_to_all | solution.py:44
  461.1 5.7 copy-start.1
  461.1 5.7 copy-start.4
  502.3 77.2 %all-to-all-start.6 = ((bf16[16,16,3,2048]{3,0,2,1:T(8,128)(2,1)}), bf16[16,16,3,2048]{3,0,2,1:T(8,128)(2,1)}, u32[]{:S(2)}, u32[]{:S(2)}) async-start(bf16[16,16,3,2048]{3,0,2,1:T(8,128)(2,1)} %copy.29), calls=%async_computation.6 | async-start | bytes 6291456 | tf_op jit(solution)/shard_map/all_to_all | solution.py:44
  579.5 53.9 %all-to-all-start.3 = ((bf16[16,16,3,2048]{3,1,2,0:T(8,128)(2,1)}), bf16[16,16,3,2048]{3,1,2,0:T(8,128)(2,1)}, u32[]{:S(2)}, u32[]{:S(2)}) async-start(bf16[16,16,3,2048]{3,1,2,0:T(8,128)(2,1)} %copy.22), calls=%async_computation.3 | async-start | bytes 6291456 | tf_op jit(solution)/shard_map/all_to_all | solution.py:45
  633.3 51.5 %all-to-all-start.7 = ((bf16[16,16,3,2048]{3,1,2,0:T(8,128)(2,1)}), bf16[16,16,3,2048]{3,1,2,0:T(8,128)(2,1)}, u32[]{:S(2)}, u32[]{:S(2)}) async-start(bf16[16,16,3,2048]{3,1,2,0:T(8,128)(2,1)} %copy.30), calls=%async_computation.7 | async-start | bytes 6291456 | tf_op jit(solution)/shard_map/all_to_all | solution.py:45
where the time goes:
time: 730 us; the launch traced here: 720 us
  waiting for transfers between devices  359 us (49%)
  local copies, waits for them, and re-layouts  232 us (32%)
  starting transfers between devices  54.9 us (8%)
  matrix products  39.9 us (5%)
  other arithmetic  32.8 us (4%)
    all_to_all x2, waiting for transfers between devices, through_owners(): lax.all_to_all(lax.all_to_all(payload, 'dp', split_axis=1, concat_axis=1,...  154 us
    all_to_all x2, waiting for transfers between devices, through_owners(): lax.all_to_all(payload, 'dp', split_axis=1, concat_axis=1, tiled=True)  87.3 us
    all_to_all x2, waiting for transfers between devices, through_owners(): lax.all_to_all(work(arrived), 'expert', split_axis=1, concat_axis=1, tile...  64.6 us
    all_to_all x2, waiting for transfers between devices, through_owners(): return lax.all_to_all(middle, 'dp', split_axis=0, concat_axis=0, tiled=True)  53.4 us
    another operation x2, local copies, waits for them, and re-layouts, body(): jnp.stack([buffer, scaled_buf]).reshape(2, n_data, n_owner, most, width)  18.2 us
    all_to_all x2, starting transfers between devices, through_owners(): lax.all_to_all(lax.all_to_all(payload, 'dp', split_axis=1, concat_axis=1,...  15.7 us
    reshape x2, local copies, waits for them, and re-layouts, body(): sent = buffer.reshape(1, n_data, n_owner, most, width)  15.5 us
    reshape x2, local copies, waits for them, and re-layouts, backward_work(): return result.reshape(shape[1:])  15.5 us
  transfers between devices with their start and end apart: 8, of which 6 were waited for; matrix products, arithmetic and copies ran while one was open for 32% of the time, Pallas kernels for 0%

commit v1 on v0

v1 whole, which is shorter than its diff:
```python
import jax
import jax.numpy as jnp
from jax import lax
from jax.sharding import PartitionSpec as P

BF = jnp.bfloat16
F32 = jnp.float32
LANES = 128


def reduce_bf16(x):
    return lax.reduce_precision(x, 8, 7)


def split_parts(x, count):
    parts = []
    for _ in range(count):
        head = reduce_bf16(x)
        parts.append(head.astype(BF))
        x = x - head
    return parts


def body(tokens, expert_ids, gate_probs, w_gate, w_up, w_down, grad_out):
    tok_dev, top = expert_ids.shape
    width = tokens.shape[1]
    n_data = lax.axis_size("dp")
    n_owner = lax.axis_size("expert")
    most = 3
    per = n_owner * most
    column = n_owner * tok_dev
    me = lax.axis_index("expert")
    wg, wu, wd = w_gate[0], w_up[0], w_down[0]

    pieces = [expert_ids.astype(BF)] + split_parts(gate_probs, 3)
    pieces.append(jnp.zeros((tok_dev, LANES - 4 * top), BF))
    meta = jnp.concatenate(pieces, axis=1)
    gathered = lax.all_gather(
        jnp.concatenate([tokens, meta], axis=1), "expert", axis=0, tiled=True
    )
    grads = lax.all_gather(grad_out, "expert", axis=0, tiled=True)
    rows = gathered[:, :width]
    info = gathered[:, width:].astype(F32)
    ids = info[:, :top].astype(jnp.int32)
    probs = info[:, top : 2 * top] + info[:, 2 * top : 3 * top] + info[:, 3 * top : 4 * top]

    mine = (ids % n_owner) == me
    place = jnp.where(mine, ids // n_owner, -1)
    hit = place[:, :, None] == jnp.arange(n_data, dtype=jnp.int32)[None, None, :]
    member = jnp.sum(hit.astype(F32), axis=1)
    weight = jnp.sum(jnp.where(hit, probs[:, :, None], 0.0), axis=1)
    lower = (jnp.arange(tok_dev)[:, None] > jnp.arange(tok_dev)[None, :]).astype(BF)
    rank = jnp.einsum(
        "ij,bjd->bid",
        lower,
        member.reshape(n_owner, tok_dev, n_data).astype(BF),
        preferred_element_type=F32,
    ).reshape(column, n_data)
    block = (jnp.arange(column, dtype=jnp.int32) // tok_dev)[:, None]
    slot = jnp.where(member > 0.0, block * most + rank.astype(jnp.int32), -1)
    select3 = slot.T[:, None, :] == jnp.arange(per, dtype=jnp.int32)[None, :, None]
    slot_prob = jnp.sum(jnp.where(select3, weight.T[:, None, :], 0.0), axis=2)
    select = select3.astype(BF).reshape(n_data * per, column)
    p_col = slot_prob.reshape(-1, 1)

    def route(x):
        y = lax.all_to_all(
            x.reshape(n_data, per, width), "dp", split_axis=0, concat_axis=0, tiled=True
        )
        return y.reshape(n_data * per, width)

    send_rows = jnp.dot(select, rows, preferred_element_type=F32).astype(BF)
    got_rows = route(send_rows)
    send_grads = (jnp.dot(select, grads, preferred_element_type=F32) * p_col).astype(BF)
    got_grads = route(send_grads)

    pre_gate = jnp.dot(got_rows, wg, preferred_element_type=F32)
    pre_up = jnp.dot(got_rows, wu, preferred_element_type=F32)
    sig = jax.nn.sigmoid(pre_gate)
    hidden = (pre_gate * sig * pre_up).astype(BF)
    result = jnp.dot(hidden, wd, preferred_element_type=F32).astype(BF)
    routed = route(result)

    last = (((1,), (1,)), ((), ()))
    grad_hidden = lax.dot_general(got_grads, wd, last, preferred_element_type=F32)
    grad_gate = (grad_hidden * pre_up * sig * (1.0 + pre_gate * (1.0 - sig))).astype(BF)
    grad_up = (grad_hidden * pre_gate * sig).astype(BF)
    back = lax.dot_general(grad_gate, wg, last, preferred_element_type=F32)
    back = back + lax.dot_general(grad_up, wu, last, preferred_element_type=F32)
    back = route(back.astype(BF))

    first = (((0,), (0,)), ((), ()))
    slot_dot = jnp.sum(send_grads.astype(F32) * routed.astype(F32), axis=1).reshape(n_data, per)
    slot_dot = jnp.where(slot_prob > 0.0, slot_dot / jnp.maximum(slot_prob, 1e-30), 0.0)
    by_place = jnp.sum(jnp.where(select3, slot_dot[:, :, None], 0.0), axis=1).T
    dots = jnp.sum(jnp.where(hit, by_place[:, None, :], 0.0), axis=2)
    combine = (select.astype(F32) * p_col).astype(BF)
    part = lax.dot_general(combine, routed, first, preferred_element_type=F32).astype(BF)
    tail = jnp.concatenate(
        split_parts(dots, 3) + [jnp.zeros((column, LANES - 3 * top), BF)], axis=1
    )
    summed = lax.psum_scatter(
        jnp.concatenate([part, tail], axis=1), "expert", scatter_dimension=0, tiled=True
    )
    mixed = summed[:, :width]
    ends = summed[:, width:].astype(F32)
    grad_probs = ends[:, :top] + ends[:, top : 2 * top] + ends[:, 2 * top : 3 * top]

    back_part = lax.dot_general(select, back, first, preferred_element_type=F32).astype(BF)
    grad_tokens = lax.psum_scatter(back_part, "expert", scatter_dimension=0, tiled=True)
    return (mixed, grad_tokens, grad_probs)


def solution(mesh):
    both = ("dp", "expert")
    return jax.shard_map(
        body,
        mesh=mesh,
        in_specs=(
            P(both, None),
            P(both, None),
            P(both, None),
            P(both, None, None),
            P(both, None, None),
            P(both, None, None),
            P(both, None),
        ),
        out_specs=(P(both, None), P(both, None), P(both, None)),
        check_vma=False,
    )
```

time: 730 us -> 345 us (0.47)
  local copies, waits for them, and re-layouts: 232 us -> 13.9 us
  waiting for transfers between devices: 359 us -> 166 us
  blocking collectives: 0 us -> 89.4 us
  starting transfers between devices: 54.9 us -> 9.31 us
  other arithmetic: 32.8 us -> 6.44 us
  between operations: 0.98 us -> 14 us
    all_to_all x8 -> x2, waiting for transfers between devices: 359 us -> 69.5 us  [route(): lax.all_to_all(x.reshape(n_data, per, width), 'dp', split_axis=0, concat_...]
    all_to_all x0 -> x2, blocking collectives: none -> 89.4 us  [route(): lax.all_to_all(x.reshape(n_data, per, width), 'dp', split_axis=0, concat_...]
    reshape x10 -> x1, local copies, waits for them, and re-layouts: 75 us -> 0.07 us  [body(): jnp.sum(send_grads.astype(F32) * routed.astype(F32), axis=1)]
    reduce_scatter x0 -> x2, waiting for transfers between devices: none -> 51.9 us  [the longest x1 51.9 us: body(): lax.psum_scatter(back_part, 'expert', scatter_dimension=0, tiled=True)]
    all_to_all x8 -> x2, starting transfers between devices: 54.9 us -> 8.96 us  [route(): lax.all_to_all(x.reshape(n_data, per, width), 'dp', split_axis=0, concat_...]
    another operation x5 -> x0, local copies, waits for them, and re-layouts: 44.7 us -> none  [the longest x2 18.2 us: body(): jnp.stack([buffer, scaled_buf]).reshape(2, n_data, n_owner, most, width)]
    all_to_all x7 -> x0, local copies, waits for them, and re-layouts: 44.5 us -> none  [the longest x2 14.1 us: through_owners(): lax.all_to_all(payload, 'dp', split_axis=1, concat_axis=1, tiled=True)]
    all_gather x0 -> x2, waiting for transfers between devices: none -> 44.1 us  [the longest x1 44.1 us: body(): lax.all_gather(jnp.concatenate([tokens, meta], axis=1), 'expert', axis=0,...]
  transfers between devices with their start and end apart: 8 -> 6, of which waited for: 6 -> 4; matrix products, arithmetic and copies ran while one was open for 32% -> 15% of each run, Pallas kernels for 0% -> 0%
where the time goes in v1:
time: 345 us; the launch traced here: 341 us
  waiting for transfers between devices  166 us (48%)
  blocking collectives  89.4 us (26%)
  matrix products  41.3 us (12%)
  between operations  14 us (4%)
  local copies, waits for them, and re-layouts  13.9 us (4%)
  starting transfers between devices  9.31 us (3%)
  other arithmetic  6.44 us (2%)
    all_to_all x2, blocking collectives, route(): lax.all_to_all(x.reshape(n_data, per, width), 'dp', split_axis=0, concat_...  89.4 us
    all_to_all x2, waiting for transfers between devices, route(): lax.all_to_all(x.reshape(n_data, per, width), 'dp', split_axis=0, concat_...  69.5 us
    reduce_scatter x1, waiting for transfers between devices, body(): lax.psum_scatter(back_part, 'expert', scatter_dimension=0, tiled=True)  51.9 us
    all_gather x1, waiting for transfers between devices, body(): lax.all_gather(jnp.concatenate([tokens, meta], axis=1), 'expert', axis=0,...  44.1 us
    all_to_all x2, starting transfers between devices, route(): lax.all_to_all(x.reshape(n_data, per, width), 'dp', split_axis=0, concat_...  8.96 us
    concatenate x1, local copies, waits for them, and re-layouts, body(): jnp.concatenate([part, tail], axis=1)  7.82 us
    dot_general x1, matrix products, body(): jnp.dot(select, grads, preferred_element_type=F32) * p_col  7.7 us
    dot_general x1, matrix products, body(): lax.dot_general(combine, routed, first, preferred_element_type=F32)  7.29 us
  transfers between devices with their start and end apart: 6, of which 4 were waited for; matrix products, arithmetic and copies ran while one was open for 15% of the time, Pallas kernels for 0%

profile of v1, /device:TPU:32, one launch (start us, length us, event | category | flops | bytes accessed | tf_op | source)
XLA Modules:
  0.0 340.7 jit_solution(9609451979330086635)
XLA Ops:
  7.2 0.8 convert_element_type.98
  8.2 0.7 fusion.34
  9.2 1.8 concatenate.6
  11.1 0.7 all-gather.5.cloned.1.call-update
  11.9 44.1 %all-gather.3.cloned.1.call-done = bf16[1024,2176]{1,0:T(8,128)(2,1)} async-done(((bf16[64,2176]{1,0:T(8,128)(2,1)}), bf16[1024,2176]{1,0:T(8,128)(2,1)}) %all-gather.3.cloned.1.call-update) | async-done | bytes 4456464 | tf_op jit(solution)/shard_map/all_gather | solution.py:38
  55.9 1.0 slice_convert_fusion.1
  56.9 0.5 slice_add_fusion
  57.4 0.5 fusion.25
  58.9 0.5 bitcast_compare_fusion
  59.4 5.8 %fusion.3 = bf16[768,2048]{1,0:T(8,128)(2,1)S(1)} fusion(pred[768,1024]{1,0:T(32,128)(4,1)S(1)} %bitcast_compare_fusion, bf16[1024,2176]{1,0:T(8,128)(2,1)} %all-gather.3.cloned.1.call-done), kind=kOutput, calls=%fused_computation.8 | convolution fusion | flops 3222798336 | bytes 8126464 | tf_op jit(solution)/shard_map/dot_general | solution.py:72
  65.2 46.8 %all_to_all.20 = bf16[16,48,2048]{2,1,0:T(8,128)(2,1)S(1)} all-to-all(bf16[16,48,2048]{2,1,0:T(8,128)(2,1)S(1)} %bitcast.56), channel_id=1, replica_groups=mesh['dp'=16,'expert'=16] {'dp'}, dimensions={0} | all-to-all | bytes 6291456 | tf_op jit(solution)/shard_map/all_to_all | solution.py:67
  112.0 1.8 fusion.15
  113.8 1.8 fusion.11
  115.6 3.5 %convolution_convert_fusion = bf16[768,2048]{1,0:T(8,128)(2,1)} fusion(bf16[1,512,2048]{2,1,0:T(8,128)(2,1)S(1)} %copy-done, f32[768,512]{1,0:T(8,128)S(1)} %fusion.11, f32[768,512]{1,0:T(8,128)S(1)} %fusion.15), kind=kOutput, calls=%fused_computation.9 | convolution fusion | flops 1614544896 | bytes 8388608 | tf_op jit(solution)/shard_map/dot_general | solution.py:81
  119.2 4.5 %all-to-all-start.1 = ((bf16[16,48,2048]{2,1,0:T(8,128)(2,1)}), bf16[16,48,2048]{2,1,0:T(8,128)(2,1)}, u32[]{:S(2)}, u32[]{:S(2)}) async-start(bf16[16,48,2048]{2,1,0:T(8,128)(2,1)} %bitcast.52), calls=%async_computation.1 | async-start | bytes 6291456 | tf_op jit(solution)/shard_map/all_to_all | solution.py:67
  123.6 0.4 select_reduce_fusion.1
  124.2 44.9 %all-to-all-done.1 = bf16[16,48,2048]{2,1,0:T(8,128)(2,1)} async-done(((bf16[16,48,2048]{2,1,0:T(8,128)(2,1)}), bf16[16,48,2048]{2,1,0:T(8,128)(2,1)}, u32[]{:S(2)}, u32[]{:S(2)}) %all-to-all-start.1) | async-done | bytes 3145760 | tf_op jit(solution)/shard_map/all_to_all | solution.py:67
  169.1 7.7 %fusion = (f32[768]{0:T(1024)S(1)}, bf16[768,2048]{1,0:T(8,128)(2,1)}) fusion(bf16[16,48,2048]{2,1,0:T(8,128)(2,1)} %all-to-all-done.1, f32[768]{0:T(1024)S(1)} %mul.63, pred[768,1024]{1,0:T(32,128)(4,1)S(1)} %bitcast_compare_fusion, bf16[1024,2048]{1,0:T(8,128)(2,1)} %all-gather.5.cloned.1.call-done), kind=kOutput, calls=%fused_computation.3 | convolution fusion | flops 3230661888 | bytes 11278336 | tf_op jit(solution)/shard_map/dot_general | solution.py:74
  176.8 4.5 %all-to-all-start.2 = ((bf16[16,48,2048]{2,1,0:T(8,128)(2,1)}), bf16[16,48,2048]{2,1,0:T(8,128)(2,1)}, u32[]{:S(2)}, u32[]{:S(2)}) async-start(bf16[16,48,2048]{2,1,0:T(8,128)(2,1)} %bitcast.51), calls=%async_computation.3 | async-start | bytes 6291456 | tf_op jit(solution)/shard_map/all_to_all | solution.py:67
  181.6 7.3 %bitcast_convert_fusion.1 = bf16[1024,2048]{1,0:T(8,128)(2,1)} fusion(bf16[16,48,2048]{2,1,0:T(8,128)(2,1)} %all-to-all-done.1, f32[16,48]{1,0:T(8,128)S(1)} %select_reduce_fusion.1, s32[16,1024]{1,0:T(8,128)S(1)} %select_bitcast_fusion), kind=kOutput, calls=%fused_computation.1 | convolution fusion | flops 3227254784 | bytes 7408640 | tf_op jit(solution)/shard_map/dot_general | solution.py:98
  188.9 0.9 select_reduce_fusion
  190.5 7.8 %concatenate.7 = bf16[1024,2176]{1,0:T(8,128)(2,1)} concatenate(bf16[1024,2048]{1,0:T(8,128)(2,1)} %bitcast_convert_fusion.1, bf16[1024,10]{1,0:T(8,128)(2,1)S(1)} %copy.49, bf16[1024,10]{1,0:T(8,128)(2,1)S(1)} %copy.50, bf16[1024,10]{1,0:T(8,128)(2,1)S(1)} %copy.51, bf16[1024,98]{1,0:T(8,128)(2,1)S(1)} %broadcast_in_dim.77), dimensions={1} | concatenate | bytes 8912896 | tf_op jit(solution)/shard_map/concatenate | solution.py:103
  198.4 24.6 %all-to-all-done.2 = bf16[16,48,2048]{2,1,0:T(8,128)(2,1)} async-done(((bf16[16,48,2048]{2,1,0:T(8,128)(2,1)}), bf16[16,48,2048]{2,1,0:T(8,128)(2,1)}, u32[]{:S(2)}, u32[]{:S(2)}) %all-to-all-start.2) | async-done | bytes 3145760 | tf_op jit(solution)/shard_map/all_to_all | solution.py:67
  223.1 3.9 %fusion.7 = f32[768,512]{1,0:T(8,128)S(1)} fusion(bf16[768,2048]{1,0:T(8,128)(2,1)} %bitcast.15, bf16[1,512,2048]{2,1,0:T(8,128)(2,1)S(1)} %copy-done), kind=kOutput, calls=%fused_computation.16 | convolution fusion | flops 1610612736 | bytes 6815744 | tf_op jit(solution)/shard_map/dot_general | solution.py:85
  227.0 2.3 fusion.13
  229.3 1.9 add_convert_fusion
  231.2 42.7 %all_to_all.21 = bf16[16,48,2048]{2,1,0:T(8,128)(2,1)S(1)} all-to-all(bf16[16,48,2048]{2,1,0:T(8,128)(2,1)S(1)} %bitcast.53), channel_id=1, replica_groups=mesh['dp'=16,'expert'=16] {'dp'}, dimensions={0} | all-to-all | bytes 6291456 | tf_op jit(solution)/shard_map/all_to_all | solution.py:67
  273.9 5.2 %bitcast_convert_fusion = bf16[1024,2048]{1,0:T(8,128)(2,1)} fusion(bf16[16,48,2048]{2,1,0:T(8,128)(2,1)S(1)} %all_to_all.21, s32[16,1024]{1,0:T(8,128)S(1)} %select_bitcast_fusion), kind=kOutput, calls=%fused_computation | convolution fusion | flops 3224109056 | bytes 7405568 | tf_op jit(solution)/shard_map/dot_general | solution.py:109
  279.1 0.7 slice_convert_fusion.2
  279.9 0.7 copy.52
  280.6 1.7 slice.50
  282.3 51.9 %reduce-scatter.5.cloned.1.call-done = bf16[64,2048]{1,0:T(8,128)(2,1)} async-done(((bf16[1024,2048]{1,0:T(8,128)(2,1)}), bf16[64,2048]{1,0:T(8,128)(2,1)}) %reduce-scatter.5.cloned.1.call-update) | async-done | bytes 262160 | tf_op jit(solution)/shard_map/reduce_scatter | solution.py:110
  (54 shorter events, 2.9 us)
Async XLA Ops:
  7.2 108.4 %copy-start = (bf16[1,512,2048]{2,1,0:T(8,128)(2,1)S(1)}, bf16[1,512,2048]{2,1,0:T(8,128)(2,1)}, u32[]{:S(2)}) copy-start(bf16[1,512,2048]{2,1,0:T(8,128)(2,1)} %param.12) | copy-start | bytes 6291460
  7.2 48.8 %all-gather.3.cloned.1.call-start = ((), (), s32[]{:S(2)}) async-start(), calls=%async_computation.6 | async-start | bytes 4734976 | tf_op jit(solution)/shard_map/all_gather | solution.py:38
  11.0 113.1 %all-gather.5.cloned.1.call-start = ((), (), s32[]{:S(2)}) async-start(), calls=%async_computation.7 | async-start | bytes 4456448 | tf_op jit(solution)/shard_map/all_gather | solution.py:41
  65.2 46.8 %copy-start.1 = (bf16[1,2048,512]{2,1,0:T(8,128)(2,1)S(1)}, bf16[1,2048,512]{2,1,0:T(8,128)(2,1)}, u32[]{:S(2)}) copy-start(bf16[1,2048,512]{2,1,0:T(8,128)(2,1)} %param.10) | copy-start | bytes 6291460
  112.0 1.8 copy-start.3
  113.8 1.8 copy-start.5
  115.6 3.5 %copy-start.7 = (f32[768,512]{1,0:T(8,128)}, f32[768,512]{1,0:T(8,128)S(1)}, u32[]{:S(2)}) copy-start(f32[768,512]{1,0:T(8,128)S(1)} %fusion.11) | copy-start | bytes 4718596
  119.2 49.9 %all-to-all-start.1 = ((bf16[16,48,2048]{2,1,0:T(8,128)(2,1)}), bf16[16,48,2048]{2,1,0:T(8,128)(2,1)}, u32[]{:S(2)}, u32[]{:S(2)}) async-start(bf16[16,48,2048]{2,1,0:T(8,128)(2,1)} %bitcast.52), calls=%async_computation.1 | async-start | bytes 6291456 | tf_op jit(solution)/shard_map/all_to_all | solution.py:67
  176.8 46.2 %all-to-all-start.2 = ((bf16[16,48,2048]{2,1,0:T(8,128)(2,1)}), bf16[16,48,2048]{2,1,0:T(8,128)(2,1)}, u32[]{:S(2)}, u32[]{:S(2)}) async-start(bf16[16,48,2048]{2,1,0:T(8,128)(2,1)} %bitcast.51), calls=%async_computation.3 | async-start | bytes 6291456 | tf_op jit(solution)/shard_map/all_to_all | solution.py:67
  181.3 97.8 %reduce-scatter.3.cloned.1.call-start = ((), (), s32[]{:S(2)}) async-start(), calls=%async_computation.8 | async-start | bytes 4734976 | tf_op jit(solution)/shard_map/reduce_scatter | solution.py:102
  198.4 135.8 %reduce-scatter.5.cloned.1.call-start = ((), (), s32[]{:S(2)}) async-start(), calls=%async_computation.9 | async-start | bytes 4456448 | tf_op jit(solution)/shard_map/reduce_scatter | solution.py:110
  223.0 3.9 %copy-start.2 = (bf16[1,2048,512]{2,1,0:T(8,128)(2,1)S(1)}, bf16[1,2048,512]{2,1,0:T(8,128)(2,1)}, u32[]{:S(2)}) copy-start(bf16[1,2048,512]{2,1,0:T(8,128)(2,1)} %param.10) | copy-start | bytes 6291460
  223.1 3.9 %copy-start.6 = (f32[768,512]{1,0:T(8,128)S(1)}, f32[768,512]{1,0:T(8,128)}, u32[]{:S(2)}) copy-start(f32[768,512]{1,0:T(8,128)} %copy-done.5) | copy-start | bytes 4718596
  223.1 3.9 %copy-start.8 = (f32[768,512]{1,0:T(8,128)S(1)}, f32[768,512]{1,0:T(8,128)}, u32[]{:S(2)}) copy-start(f32[768,512]{1,0:T(8,128)} %copy-done.7) | copy-start | bytes 4718596
  227.0 2.3 copy-start.4
Sparse Core Ops, SparseCore 0:
  11.1 44.7 all-gather.2
  57.8 40.7 all-gather.4
  198.5 60.2 reduce-scatter.2
  279.2 54.9 reduce-scatter.4
